TPU v7x, 32 devices: a whole 2x2x4 slice. The times are simulated.
32 devices in a mesh: coil: 4 (over y, core), slab: 8 (over z, x).
Axes of the slice: x: 2, y: 2, z: 4, core: 2. Of those that a mesh axis runs over, the one named last changes fastest.
Arguments:
- image: float32 [2, 3, 512, 512], P(None, None, 'slab'), may hold values from -6 to 6
- sens: float32 [2, 8, 3, 512, 512], P(None, 'coil', None, 'slab'), may hold values from -2 to 2
- kdata: float32 [2, 8, 3, 512, 512], P(None, 'coil', None, 'slab'), may hold values from -6 to 6
- mask: int32 [512, 512], P('slab'), may hold values 0 or 1
- threshold: float32 [3], replicated, may hold values from 0.1 to 1
Outputs:
- updated: float32 [2, 3, 512, 512], P(None, None, 'slab')
All inputs are finite; a program needn't handle non-finite values. No bound on the sum of `mask` on one device may be relied on, other than what follows from the above.
Results may differ from a plain program's by a relative error of at most 0.0001.
Values sent between devices are 32-bit elements; how exact they have to be, the bound alone decides.
A program may use at most 64 MiB of HBM per device.

v0:
```python
import functools
import math

import jax
import jax.numpy as jnp
import ml_dtypes
import numpy as np
from jax import lax
from jax.experimental import pallas as pl
from jax.experimental.pallas import tpu as pltpu
from jax.sharding import PartitionSpec as P

LEVELS = 3
HALO = 16
MESH = pl.DeviceIdType.MESH

root_three = math.sqrt(3.0)
norm_four = 4.0 * math.sqrt(2.0)
low_taps = (
    (1.0 + root_three) / norm_four,
    (3.0 + root_three) / norm_four,
    (3.0 - root_three) / norm_four,
    (1.0 - root_three) / norm_four,
)
high_taps = (low_taps[3], -low_taps[2], low_taps[1], -low_taps[0])


def halves(table):
    top = table.astype(np.float32).astype(ml_dtypes.bfloat16)
    rest = (table - top.astype(np.float64)).astype(np.float32).astype(ml_dtypes.bfloat16)
    return np.stack([top, rest])


def fourier(length):
    places = np.arange(length)
    angle = (places[:, None] * places[None, :] % length) * (2.0 * np.pi / length)
    factor = 1.0 / math.sqrt(length)
    return halves(np.cos(angle) * factor), halves(np.sin(angle) * factor)


def one_level(length, wrap):
    low, high = np.zeros((length // 2, length)), np.zeros((length // 2, length))
    for i in range(length // 2):
        for k in range(4):
            at = 2 * i + k
            if at >= length:
                if not wrap:
                    continue
                at %= length
            low[i, at] += low_taps[k]
            high[i, at] += high_taps[k]
    return low, high


def all_levels(length, wrap):
    reach, found = np.eye(length), []
    for _ in range(LEVELS):
        low, high = one_level(reach.shape[0], wrap)
        found.append(np.concatenate([low @ reach, high @ reach]))
        reach = low @ reach
    return found


def thrice(values, table):
    top = values.astype(jnp.bfloat16)
    rest = (values - top.astype(jnp.float32)).astype(jnp.bfloat16)
    dot = functools.partial(jnp.dot, preferred_element_type=jnp.float32)
    return dot(top, table[0]) + (dot(rest, table[0]) + dot(top, table[1]))


def dft(re, im, cos, sin, sign):
    rows = re.shape[0]
    both = jnp.concatenate([re, im], axis=0)
    by_cos, by_sin = thrice(both, cos), thrice(both, sin)
    if sign < 0:
        return by_cos[:rows] + by_sin[rows:], by_cos[rows:] - by_sin[:rows]
    return by_cos[:rows] - by_sin[rows:], by_cos[rows:] + by_sin[:rows]


def exactly(left, right):
    return jnp.dot(left, right, precision=lax.Precision.HIGHEST, preferred_element_type=jnp.float32)


def kernel(
    sizes, thr, image, sens, kdata, mask, cos, sin, cols, cols_t, *refs
):
    slabs, groups, coils, planes, rows, own, length1, length2 = sizes
    down, up, refs = refs[:LEVELS], refs[LEVELS:2 * LEVELS], refs[2 * LEVELS:]
    (out, front, front_in, rear, rear_in, terms, window,
     fs_sem, fr_sem, rs_sem, rr_sem, ts_sem, tr_sem, hs_sem, hr_sem) = refs
    me = lax.axis_index("slab")
    group = lax.axis_index("coil")
    total_rows = rows + 2 * HALO

    barrier = pltpu.get_barrier_semaphore()
    for k in range(1, slabs):
        pl.semaphore_signal(barrier, inc=1, device_id={"slab": lax.rem(me + k, slabs)}, device_id_type=MESH)
    for k in range(1, groups):
        pl.semaphore_signal(barrier, inc=1, device_id={"coil": lax.rem(group + k, groups)}, device_id_type=MESH)
    pl.semaphore_wait(barrier, slabs - 1 + groups - 1)

    def swap(r, k, source, target, send, recv):
        to = lax.rem(me + k, slabs)
        return pltpu.make_async_remote_copy(
            src_ref=source.at[r, to],
            dst_ref=target.at[r, me],
            send_sem=send.at[r, k],
            recv_sem=recv.at[r, k],
            device_id={"slab": to},
            device_id_type=MESH,
        )

    def share(r, k):
        return pltpu.make_async_remote_copy(
            src_ref=terms.at[r, group],
            dst_ref=terms.at[r, group],
            send_sem=ts_sem.at[r, k],
            recv_sem=tr_sem.at[r, k],
            device_id={"coil": lax.rem(group + k, groups)},
            device_id_type=MESH,
        )

    def edge(r, way):
        if way == 0:
            to, at, there = lax.rem(me + slabs - 1, slabs), HALO, HALO + rows
        else:
            to, at, there = lax.rem(me + 1, slabs), rows, 0
        return pltpu.make_async_remote_copy(
            src_ref=window.at[r, :, pl.ds(at, HALO), :],
            dst_ref=window.at[r, :, pl.ds(there, HALO), :],
            send_sem=hs_sem.at[r, way],
            recv_sem=hr_sem.at[r, way],
            device_id={"slab": to},
            device_id_type=MESH,
        )

    def scatter(r, re, im, height, width, source, target, send, recv):
        for d in range(slabs):
            cut = slice(d * width, (d + 1) * width)
            block = jnp.concatenate([re[:, cut], im[:, cut]], axis=1)
            source[r, d] = block.reshape(coils, height, 2 * width)
        target[r, me] = source[r, me]
        for k in range(1, slabs):
            swap(r, k, source, target, send, recv).start()

    def gather(r, width, source, target, send, recv):
        for k in range(1, slabs):
            swap(r, k, source, target, send, recv).wait_recv()
        re, im = [], []
        for c in range(coils):
            block = target[r, :, c]
            turned = block.reshape(block.shape[0] * block.shape[1], 2 * width).T
            re.append(turned[:width])
            im.append(turned[width:])
        return jnp.concatenate(re, axis=0), jnp.concatenate(im, axis=0)

    def stage_a(r):
        re, im = [], []
        for c in range(coils):
            s_re, s_im = sens[0, c, r], sens[1, c, r]
            re.append(s_re * image[0, r] - s_im * image[1, r])
            im.append(s_re * image[1, r] + s_im * image[0, r])
        re, im = dft(jnp.concatenate(re, axis=0), jnp.concatenate(im, axis=0), cos, sin, -1)
        scatter(r, re, im, rows, own, front, front_in, fs_sem, fr_sem)

    def stage_b(r):
        re, im = gather(r, own, front, front_in, fs_sem, fr_sem)
        re, im = dft(re, im, cos, sin, -1)
        live = jnp.concatenate([mask[...].astype(jnp.float32)] * coils, axis=0)
        y_re = jnp.concatenate([kdata[0, c, r] for c in range(coils)], axis=0)
        y_im = jnp.concatenate([kdata[1, c, r] for c in range(coils)], axis=0)
        re, im = dft(live * (re - y_re), live * (im - y_im), cos, sin, 1)
        scatter(r, re, im, own, rows, rear, rear_in, rs_sem, rr_sem)

    def stage_c(r):
        re, im = gather(r, rows, rear, rear_in, rs_sem, rr_sem)
        re, im = dft(re, im, cos, sin, 1)
        grad_re = grad_im = 0.0
        for c in range(coils):
            cut = slice(c * rows, (c + 1) * rows)
            s_re, s_im = sens[0, c, r], sens[1, c, r]
            grad_re += s_re * re[cut] + s_im * im[cut]
            grad_im += s_re * im[cut] - s_im * re[cut]
        terms[r, group, 0] = grad_re
        terms[r, group, 1] = grad_im
        for k in range(1, groups):
            share(r, k).start()

    def stage_d(r):
        for k in range(1, groups):
            share(r, k).wait()
        total = terms[r, 0]
        for g in range(1, groups):
            total = total + terms[r, g]
        window[r, :, HALO:HALO + rows] = image[:, r] - total
        for way in (0, 1):
            edge(r, way).start()

    def stage_e(r):
        for way in (0, 1):
            edge(r, way).wait()
        limit = thr[r]
        full = window[r].reshape(2 * total_rows, length2)
        split = thrice(full, cols)
        joined = ([], [])
        first = 0
        for level in range(LEVELS):
            width = length2 >> level
            high = total_rows >> level
            pair = []
            for p in range(2):
                part = split[p * total_rows:(p + 1) * total_rows, first:first + width]
                pair.append(exactly(down[level][...], part))
            shape = pair[0].shape
            low_low = (lax.broadcasted_iota(jnp.int32, shape, 0) < high // 2) & (
                lax.broadcasted_iota(jnp.int32, shape, 1) < width // 2
            )
            magnitude = jnp.sqrt(pair[0] * pair[0] + pair[1] * pair[1])
            factor = jnp.maximum(magnitude - limit, 0.0) / jnp.maximum(magnitude, limit)
            factor = jnp.where(low_low, 1.0 if level == LEVELS - 1 else 0.0, factor)
            for p in range(2):
                joined[p].append(exactly(up[level][...], pair[p] * factor))
            first += width
        whole = jnp.concatenate([jnp.concatenate(joined[p], axis=1) for p in range(2)], axis=0)
        out[:, r] = thrice(whole, cols_t).reshape(2, rows, length2)

    def loop(count, body):
        def step(t, carry):
            body(t)
            return carry

        lax.fori_loop(0, count, step, 0)

    loop(planes, stage_a)
    loop(planes, stage_b)

    def tail(t):
        pl.when(t < planes)(lambda: stage_c(t))
        pl.when((t >= 2) & (t < planes + 2))(lambda: stage_e(t - 2))
        pl.when((t >= 1) & (t < planes + 1))(lambda: stage_d(t - 1))

    loop(planes + 2, tail)

    def drain(r):
        for k in range(1, slabs):
            swap(r, k, front, front_in, fs_sem, fr_sem).wait_send()
            swap(r, k, rear, rear_in, rs_sem, rr_sem).wait_send()

    loop(planes, drain)


def shards(image, sens, kdata, mask, threshold):
    slabs, groups = lax.axis_size("slab"), lax.axis_size("coil")
    _, coils, planes, rows, length2 = sens.shape
    own, length1 = kdata.shape[3:]
    total_rows = rows + 2 * HALO
    cos, sin = fourier(length2)
    cols = np.concatenate(all_levels(length2, True), axis=0)
    down, up = [], []
    for matrix in all_levels(total_rows, False):
        matrix = np.pad(matrix, ((0, -matrix.shape[0] % 8), (0, 0))).astype(np.float32)
        down.append(matrix)
        up.append(np.ascontiguousarray(matrix[:, HALO:HALO + rows].T))
    sizes = (slabs, groups, coils, planes, rows, own, length1, length2)
    operands = [threshold, image, sens, kdata, mask, cos, sin,
                halves(np.ascontiguousarray(cols.T)), halves(cols), *down, *up]
    operands = [jnp.asarray(x) for x in operands]
    f32 = jnp.float32
    dma = pltpu.SemaphoreType.DMA
    front = pltpu.VMEM((planes, slabs, coils, rows, 2 * own), f32)
    rear = pltpu.VMEM((planes, slabs, coils, own, 2 * rows), f32)
    return pl.pallas_call(
        functools.partial(kernel, sizes),
        out_shape=jax.ShapeDtypeStruct(image.shape, f32),
        in_specs=[pl.BlockSpec(memory_space=pltpu.SMEM)]
        + [pl.BlockSpec(memory_space=pltpu.VMEM)] * (len(operands) - 1),
        out_specs=pl.BlockSpec(memory_space=pltpu.VMEM),
        scratch_shapes=[
            front, front, rear, rear,
            pltpu.VMEM((planes, groups, 2, rows, length2), f32),
            pltpu.VMEM((planes, 2, total_rows, length2), f32),
            dma((planes, slabs)), dma((planes, slabs)),
            dma((planes, slabs)), dma((planes, slabs)),
            dma((planes, groups)), dma((planes, groups)),
            dma((planes, 2)), dma((planes, 2)),
        ],
        compiler_params=pltpu.CompilerParams(
            collective_id=0, has_side_effects=True, vmem_limit_bytes=48 * 2**20
        ),
    )(*operands)


def solution(mesh):
    in_specs = (
        P(None, None, "slab", None),
        P(None, "coil", None, "slab", None),
        P(None, "coil", None, "slab", None),
        P("slab", None),
        P(),
    )
    out_specs = P(None, None, "slab", None)
    return jax.shard_map(shards, mesh=mesh, in_specs=in_specs, out_specs=out_specs, check_vma=False)
```

profile of v0, /device:TPU:1, one launch (start us, length us, event | category | flops | bytes accessed | tf_op | source)
XLA Modules:
  0.0 123.3 jit_solution(3693995534237998910)
XLA Ops:
  0.0 0.0 copy-start
  0.0 1.4 %copy-done = f32[2,2,3,64,512]{4,3,2,1,0:T(8,128)S(1)} copy-done((f32[2,2,3,64,512]{4,3,2,1,0:T(8,128)S(1)}, f32[2,2,3,64,512]{4,3,2,1,0:T(8,128)}, u32[]{:S(2)}) %copy-start) | copy-done | bytes 1572888
  1.4 0.0 copy-start.1
  1.4 1.2 copy-done.1
  2.6 0.0 copy-start.2
  2.6 1.2 copy-done.2
  3.9 0.0 copy-start.3
  3.9 1.1 copy-done.3
  5.0 0.0 copy-start.4
  5.0 0.9 copy-done.4
  5.9 0.0 copy-start.5
  5.9 0.8 copy-done.5
  6.7 0.0 copy-start.6
  6.7 0.8 copy-done.6
  7.5 0.0 copy-start.7
  7.5 0.8 copy-done.7
  8.2 0.0 copy-start.8
  8.2 0.8 copy-done.8
  9.0 0.0 copy-start.9
  9.0 0.7 copy-done.9
  9.7 0.0 copy-start.10
  9.7 0.7 copy-done.10
  10.4 0.0 copy-start.11
  10.4 0.7 copy-done.11
  11.1 111.4 %shard_map.145 = f32[2,3,64,512]{3,2,1,0:T(8,128)S(1)} custom-call(f32[3]{0:T(128)S(1)} %copy-done.11, f32[2,3,64,512]{3,2,1,0:T(8,128)S(1)} %copy-done.3, f32[2,2,3,64,512]{4,3,2,1,0:T(8,128)S(1)} %copy-done, f32[2,2,3,64,512]{4,3,2,1,0:T(8,128)} %kdata.1, s32[64,512]{1,0:T(8,128)S(1)} %copy-done.4, bf16[2,512,512]{2,1,0:T(8,128)(2,1)S(1)} %copy-done.2, ...), custom_call_target="tpu_custom_call" | custom-call | tf_op jit(solution)/shard_map/pallas_call | solution.py:272
  122.4 0.9 copy.17
Async XLA Ops:
  0.0 1.4 %copy-start = (f32[2,2,3,64,512]{4,3,2,1,0:T(8,128)S(1)}, f32[2,2,3,64,512]{4,3,2,1,0:T(8,128)}, u32[]{:S(2)}) copy-start(f32[2,2,3,64,512]{4,3,2,1,0:T(8,128)} %sens.1) | copy-start | bytes 4718596
  1.4 1.2 copy-start.1
  2.6 1.2 copy-start.2
  3.9 1.1 copy-start.3
  5.0 0.9 copy-start.4
  5.9 0.8 copy-start.5
  6.7 0.8 copy-start.6
  7.5 0.8 copy-start.7
  8.2 0.8 copy-start.8
  9.0 0.7 copy-start.9
  9.7 0.7 copy-start.10
  10.4 0.7 copy-start.11
where the time goes:
time: 124 us; the launch traced here: 123 us
  Pallas kernels  111 us (90%)
  local copies, waits for them, and re-layouts  11.9 us (10%)
    pallas_call x1, Pallas kernels, shards(): pl.pallas_call(functools.partial(kernel, sizes), out_shape=jax.ShapeDtype...  111 us
    unnamed x25, local copies, waits for them, and re-layouts  11.9 us

commit v1 on v0

--- a/solution.py
+++ b/solution.py
@@ -82,12 +82,23 @@
 
 
 def kernel(
-    sizes, thr, image, sens, kdata, mask, cos, sin, cols, cols_t, *refs
+    sizes, thr, *refs
 ):
     slabs, groups, coils, planes, rows, own, length1, length2 = sizes
-    down, up, refs = refs[:LEVELS], refs[LEVELS:2 * LEVELS], refs[2 * LEVELS:]
-    (out, front, front_in, rear, rear_in, terms, window,
-     fs_sem, fr_sem, rs_sem, rr_sem, ts_sem, tr_sem, hs_sem, hr_sem) = refs
+    count = 8 + 2 * LEVELS
+    far, out, near, refs = refs[:count], refs[count], refs[count + 1:2 * count + 1], refs[2 * count + 1:]
+    image, sens, kdata, mask, cos, sin, cols, cols_t = near[:8]
+    down, up = near[8:8 + LEVELS], near[8 + LEVELS:]
+    (front, front_in, rear, rear_in, terms, pieces, window, load_sem,
+     fs_sem, fr_sem, rs_sem, rr_sem, ts_sem, tr_sem, gs_sem, gr_sem, hs_sem, hr_sem) = refs
+    piece = pieces.shape[3]
+
+    def load(i):
+        return pltpu.make_async_copy(far[i], near[i], load_sem.at[i])
+
+    for i in (0, 1, 4, 5, 2, 3, *range(6, count)):
+        load(i).start()
+
     me = lax.axis_index("slab")
     group = lax.axis_index("coil")
     total_rows = rows + 2 * HALO
@@ -111,14 +122,32 @@
         )
 
     def share(r, k):
+        to = lax.rem(group + k, groups)
         return pltpu.make_async_remote_copy(
-            src_ref=terms.at[r, group],
-            dst_ref=terms.at[r, group],
+            src_ref=terms.at[r, :, cut_of(to), :],
+            dst_ref=pieces.at[r, group],
             send_sem=ts_sem.at[r, k],
             recv_sem=tr_sem.at[r, k],
+            device_id={"coil": to},
+            device_id_type=MESH,
+        )
+
+    def spread(r, k):
+        place = window.at[r, :, pl.ds(pl.multiple_of(HALO + start_of(group), 8), piece), :]
+        return pltpu.make_async_remote_copy(
+            src_ref=place,
+            dst_ref=place,
+            send_sem=gs_sem.at[r, k],
+            recv_sem=gr_sem.at[r, k],
             device_id={"coil": lax.rem(group + k, groups)},
             device_id_type=MESH,
         )
+
+    def start_of(g):
+        return g * piece if piece < rows else 0
+
+    def cut_of(g):
+        return pl.ds(pl.multiple_of(start_of(g), 8), piece)
 
     def edge(r, way):
         if way == 0:
@@ -181,18 +210,28 @@
             s_re, s_im = sens[0, c, r], sens[1, c, r]
             grad_re += s_re * re[cut] + s_im * im[cut]
             grad_im += s_re * im[cut] - s_im * re[cut]
-        terms[r, group, 0] = grad_re
-        terms[r, group, 1] = grad_im
+        terms[r, 0] = grad_re
+        terms[r, 1] = grad_im
+        pieces[r, group] = terms[r, :, cut_of(group), :]
         for k in range(1, groups):
             share(r, k).start()
 
     def stage_d(r):
         for k in range(1, groups):
             share(r, k).wait()
-        total = terms[r, 0]
+        total = pieces[r, 0]
         for g in range(1, groups):
-            total = total + terms[r, g]
-        window[r, :, HALO:HALO + rows] = image[:, r] - total
+            total = total + pieces[r, g]
+        moved = image[:, r, cut_of(group), :] - total
+        window[r, :, pl.ds(pl.multiple_of(HALO + start_of(group), 8), piece), :] = moved
+        if piece < rows:
+            for k in range(1, groups):
+                spread(r, k).start()
+
+    def stage_edges(r):
+        if piece < rows:
+            for k in range(1, groups):
+                spread(r, k).wait()
         for way in (0, 1):
             edge(r, way).start()
 
@@ -231,15 +270,22 @@
 
         lax.fori_loop(0, count, step, 0)
 
+    for i in (0, 1, 4, 5):
+        load(i).wait()
     loop(planes, stage_a)
+    for i in (2, 3):
+        load(i).wait()
     loop(planes, stage_b)
+    for i in range(6, count):
+        load(i).wait()
 
     def tail(t):
         pl.when(t < planes)(lambda: stage_c(t))
-        pl.when((t >= 2) & (t < planes + 2))(lambda: stage_e(t - 2))
+        pl.when(t >= 3)(lambda: stage_e(t - 3))
         pl.when((t >= 1) & (t < planes + 1))(lambda: stage_d(t - 1))
-
-    loop(planes + 2, tail)
+        pl.when((t >= 2) & (t < planes + 2))(lambda: stage_edges(t - 2))
+
+    loop(planes + 3, tail)
 
     def drain(r):
         for k in range(1, slabs):
@@ -266,6 +312,7 @@
                 halves(np.ascontiguousarray(cols.T)), halves(cols), *down, *up]
     operands = [jnp.asarray(x) for x in operands]
     f32 = jnp.float32
+    piece = rows // groups if rows % (8 * groups) == 0 else rows
     dma = pltpu.SemaphoreType.DMA
     front = pltpu.VMEM((planes, slabs, coils, rows, 2 * own), f32)
     rear = pltpu.VMEM((planes, slabs, coils, own, 2 * rows), f32)
@@ -273,19 +320,22 @@
         functools.partial(kernel, sizes),
         out_shape=jax.ShapeDtypeStruct(image.shape, f32),
         in_specs=[pl.BlockSpec(memory_space=pltpu.SMEM)]
-        + [pl.BlockSpec(memory_space=pltpu.VMEM)] * (len(operands) - 1),
+        + [pl.BlockSpec(memory_space=pl.ANY)] * (len(operands) - 1),
         out_specs=pl.BlockSpec(memory_space=pltpu.VMEM),
-        scratch_shapes=[
+        scratch_shapes=[pltpu.VMEM(x.shape, x.dtype) for x in operands[1:]] + [
             front, front, rear, rear,
-            pltpu.VMEM((planes, groups, 2, rows, length2), f32),
+            pltpu.VMEM((planes, 2, rows, length2), f32),
+            pltpu.VMEM((planes, groups, 2, piece, length2), f32),
             pltpu.VMEM((planes, 2, total_rows, length2), f32),
+            dma((len(operands) - 1,)),
             dma((planes, slabs)), dma((planes, slabs)),
             dma((planes, slabs)), dma((planes, slabs)),
+            dma((planes, groups)), dma((planes, groups)),
             dma((planes, groups)), dma((planes, groups)),
             dma((planes, 2)), dma((planes, 2)),
         ],
         compiler_params=pltpu.CompilerParams(
-            collective_id=0, has_side_effects=True, vmem_limit_bytes=48 * 2**20
+            collective_id=0, has_side_effects=True, vmem_limit_bytes=60 * 2**20
         ),
     )(*operands)
 

time: 124 us -> 106 us (0.85)
  local copies, waits for them, and re-layouts: 11.9 us -> 2.1 us
  Pallas kernels: 111 us -> 102 us
    unnamed x25 -> x1, local copies, waits for them, and re-layouts: 11.9 us -> 2.1 us
    pallas_call x1, Pallas kernels: 111 us -> 102 us  [shards(): pl.pallas_call(functools.partial(kernel, sizes), out_shape=jax.ShapeDtype...]
where the time goes in v1:
time: 106 us; the launch traced here: 104 us
  Pallas kernels  102 us (96%)
  local copies, waits for them, and re-layouts  2.1 us (2%)
    pallas_call x1, Pallas kernels, shards(): pl.pallas_call(functools.partial(kernel, sizes), out_shape=jax.ShapeDtype...  102 us

profile of v1, /device:TPU:1, one launch (start us, length us, event | category | flops | bytes accessed | tf_op | source)
XLA Modules:
  0.0 104.3 jit_solution(105907962613011932)
XLA Ops:
  0.0 102.2 %shard_map.145 = f32[2,3,64,512]{3,2,1,0:T(8,128)} custom-call(f32[3]{0:T(128)} %thr.1, f32[2,3,64,512]{3,2,1,0:T(8,128)} %refs_0_.1, f32[2,2,3,64,512]{4,3,2,1,0:T(8,128)} %refs_1_.1, f32[2,2,3,64,512]{4,3,2,1,0:T(8,128)} %refs_2_.1, s32[64,512]{1,0:T(8,128)} %refs_3_.1, bf16[2,512,512]{2,1,0:T(8,128)(2,1)} %constant.20.clone.refs_4_, ...), custom_call_target="tpu_custom_call" | custom-call | tf_op jit(solution)/shard_map/pallas_call | solution.py:319
  102.2 2.1 %copy.17 = f32[2,3,64,512]{3,2,1,0:T(8,128)} copy(f32[2,3,64,512]{3,2,1,0:T(8,128)} %shard_map.145) | data formatting | bytes 1572864

commit v2 on v1

--- a/solution.py
+++ b/solution.py
@@ -77,8 +77,11 @@
     return by_cos[:rows] - by_sin[rows:], by_cos[rows:] + by_sin[:rows]
 
 
-def exactly(left, right):
-    return jnp.dot(left, right, precision=lax.Precision.HIGHEST, preferred_element_type=jnp.float32)
+def thrice_left(left, values):
+    top = values.astype(jnp.bfloat16)
+    rest = (values - top.astype(jnp.float32)).astype(jnp.bfloat16)
+    deep = jnp.concatenate([top, rest, top], axis=0)
+    return jnp.dot(left, deep, preferred_element_type=jnp.float32)
 
 
 def kernel(
@@ -92,6 +95,7 @@
     (front, front_in, rear, rear_in, terms, pieces, window, load_sem,
      fs_sem, fr_sem, rs_sem, rr_sem, ts_sem, tr_sem, gs_sem, gr_sem, hs_sem, hr_sem) = refs
     piece = pieces.shape[3]
+    fold = HALO <= piece < rows
 
     def load(i):
         return pltpu.make_async_copy(far[i], near[i], load_sem.at[i])
@@ -108,7 +112,12 @@
         pl.semaphore_signal(barrier, inc=1, device_id={"slab": lax.rem(me + k, slabs)}, device_id_type=MESH)
     for k in range(1, groups):
         pl.semaphore_signal(barrier, inc=1, device_id={"coil": lax.rem(group + k, groups)}, device_id_type=MESH)
-    pl.semaphore_wait(barrier, slabs - 1 + groups - 1)
+    if fold:
+        for k in range(1, groups):
+            for s in (1, slabs - 1):
+                beside = {"slab": lax.rem(me + s, slabs), "coil": lax.rem(group + k, groups)}
+                pl.semaphore_signal(barrier, inc=1, device_id=beside, device_id_type=MESH)
+    pl.semaphore_wait(barrier, slabs - 1 + (3 if fold else 1) * (groups - 1))
 
     def swap(r, k, source, target, send, recv):
         to = lax.rem(me + k, slabs)
@@ -149,7 +158,7 @@
     def cut_of(g):
         return pl.ds(pl.multiple_of(start_of(g), 8), piece)
 
-    def edge(r, way):
+    def edge(r, way, coil=None):
         if way == 0:
             to, at, there = lax.rem(me + slabs - 1, slabs), HALO, HALO + rows
         else:
@@ -157,11 +166,18 @@
         return pltpu.make_async_remote_copy(
             src_ref=window.at[r, :, pl.ds(at, HALO), :],
             dst_ref=window.at[r, :, pl.ds(there, HALO), :],
-            send_sem=hs_sem.at[r, way],
+            send_sem=hs_sem.at[r, way, 0 if coil is None else coil],
             recv_sem=hr_sem.at[r, way],
-            device_id={"slab": to},
+            device_id={"slab": to} if coil is None else {"slab": to, "coil": coil},
             device_id_type=MESH,
         )
+
+    def edges(r, act):
+        for way, owner in ((0, 0), (1, groups - 1)):
+            @pl.when(group == owner)
+            def _():
+                for coil in range(groups):
+                    act(edge(r, way, coil))
 
     def scatter(r, re, im, height, width, source, target, send, recv):
         for d in range(slabs):
@@ -227,8 +243,12 @@
         if piece < rows:
             for k in range(1, groups):
                 spread(r, k).start()
+        if fold:
+            edges(r, lambda copy: copy.start())
 
     def stage_edges(r):
+        if fold:
+            return
         if piece < rows:
             for k in range(1, groups):
                 spread(r, k).wait()
@@ -236,8 +256,14 @@
             edge(r, way).start()
 
     def stage_e(r):
+        if fold:
+            for k in range(1, groups):
+                spread(r, k).wait()
         for way in (0, 1):
-            edge(r, way).wait()
+            if fold:
+                edge(r, way).wait_recv()
+            else:
+                edge(r, way).wait()
         limit = thr[r]
         full = window[r].reshape(2 * total_rows, length2)
         split = thrice(full, cols)
@@ -249,7 +275,7 @@
             pair = []
             for p in range(2):
                 part = split[p * total_rows:(p + 1) * total_rows, first:first + width]
-                pair.append(exactly(down[level][...], part))
+                pair.append(thrice_left(down[level][...], part))
             shape = pair[0].shape
             low_low = (lax.broadcasted_iota(jnp.int32, shape, 0) < high // 2) & (
                 lax.broadcasted_iota(jnp.int32, shape, 1) < width // 2
@@ -258,7 +284,7 @@
             factor = jnp.maximum(magnitude - limit, 0.0) / jnp.maximum(magnitude, limit)
             factor = jnp.where(low_low, 1.0 if level == LEVELS - 1 else 0.0, factor)
             for p in range(2):
-                joined[p].append(exactly(up[level][...], pair[p] * factor))
+                joined[p].append(thrice_left(up[level][...], pair[p] * factor))
             first += width
         whole = jnp.concatenate([jnp.concatenate(joined[p], axis=1) for p in range(2)], axis=0)
         out[:, r] = thrice(whole, cols_t).reshape(2, rows, length2)
@@ -281,16 +307,20 @@
 
     def tail(t):
         pl.when(t < planes)(lambda: stage_c(t))
-        pl.when(t >= 3)(lambda: stage_e(t - 3))
         pl.when((t >= 1) & (t < planes + 1))(lambda: stage_d(t - 1))
-        pl.when((t >= 2) & (t < planes + 2))(lambda: stage_edges(t - 2))
-
-    loop(planes + 3, tail)
+        if not fold:
+            pl.when((t >= 2) & (t < planes + 2))(lambda: stage_edges(t - 2))
+        pl.when(t >= late)(lambda: stage_e(t - late))
+
+    late = 2 if fold else 3
+    loop(planes + late, tail)
 
     def drain(r):
         for k in range(1, slabs):
             swap(r, k, front, front_in, fs_sem, fr_sem).wait_send()
             swap(r, k, rear, rear_in, rs_sem, rr_sem).wait_send()
+        if fold:
+            edges(r, lambda copy: copy.wait_send())
 
     loop(planes, drain)
 
@@ -304,9 +334,10 @@
     cols = np.concatenate(all_levels(length2, True), axis=0)
     down, up = [], []
     for matrix in all_levels(total_rows, False):
-        matrix = np.pad(matrix, ((0, -matrix.shape[0] % 8), (0, 0))).astype(np.float32)
-        down.append(matrix)
-        up.append(np.ascontiguousarray(matrix[:, HALO:HALO + rows].T))
+        matrix = np.pad(matrix, ((0, -matrix.shape[0] % 16), (0, 0)))
+        for kept, table in ((down, matrix), (up, matrix[:, HALO:HALO + rows].T)):
+            top, rest = halves(table)
+            kept.append(np.concatenate([top, top, rest], axis=1))
     sizes = (slabs, groups, coils, planes, rows, own, length1, length2)
     operands = [threshold, image, sens, kdata, mask, cos, sin,
                 halves(np.ascontiguousarray(cols.T)), halves(cols), *down, *up]
@@ -332,7 +363,7 @@
             dma((planes, slabs)), dma((planes, slabs)),
             dma((planes, groups)), dma((planes, groups)),
             dma((planes, groups)), dma((planes, groups)),
-            dma((planes, 2)), dma((planes, 2)),
+            dma((planes, 2, groups)), dma((planes, 2)),
         ],
         compiler_params=pltpu.CompilerParams(
             collective_id=0, has_side_effects=True, vmem_limit_bytes=60 * 2**20

time: 106 us -> 102 us (0.962); the launches traced: 104 us -> 101 us
  Pallas kernels: 102 us -> 99.3 us
    pallas_call x1, Pallas kernels: 102 us -> 99.3 us  [shards(): pl.pallas_call(functools.partial(kernel, sizes), out_shape=jax.ShapeDtype...]
where the time goes in v2:
time: 102 us; the launch traced here: 101 us
  Pallas kernels  99.3 us (97%)
  local copies, waits for them, and re-layouts  2.1 us (2%)
    pallas_call x1, Pallas kernels, shards(): pl.pallas_call(functools.partial(kernel, sizes), out_shape=jax.ShapeDtype...  99.3 us
    unnamed x1, local copies, waits for them, and re-layouts  2.1 us

profile of v2, /device:TPU:1, one launch (start us, length us, event | category | flops | bytes accessed | tf_op | source)
XLA Modules:
  0.0 101.4 jit_solution(15762868165620783458)
XLA Ops:
  0.0 99.3 %shard_map.145 = f32[2,3,64,512]{3,2,1,0:T(8,128)} custom-call(f32[3]{0:T(128)} %thr.1, f32[2,3,64,512]{3,2,1,0:T(8,128)} %refs_0_.1, f32[2,2,3,64,512]{4,3,2,1,0:T(8,128)} %refs_1_.1, f32[2,2,3,64,512]{4,3,2,1,0:T(8,128)} %refs_2_.1, s32[64,512]{1,0:T(8,128)} %refs_3_.1, bf16[2,512,512]{2,1,0:T(8,128)(2,1)} %constant.20.clone.refs_4_, ...), custom_call_target="tpu_custom_call" | custom-call | tf_op jit(solution)/shard_map/pallas_call | solution.py:350
  99.3 2.1 %copy.17 = f32[2,3,64,512]{3,2,1,0:T(8,128)} copy(f32[2,3,64,512]{3,2,1,0:T(8,128)} %shard_map.145) | data formatting | bytes 1572864

commit v3 on v2

--- a/solution.py
+++ b/solution.py
@@ -185,7 +185,7 @@
             block = jnp.concatenate([re[:, cut], im[:, cut]], axis=1)
             source[r, d] = block.reshape(coils, height, 2 * width)
         target[r, me] = source[r, me]
-        for k in range(1, slabs):
+        for k in sorted(range(1, slabs), key=lambda k: abs(2 * k - slabs)):
             swap(r, k, source, target, send, recv).start()
 
     def gather(r, width, source, target, send, recv):

time: 102 us -> 98.4 us (0.965); the launches traced: 101 us -> 96.5 us
  Pallas kernels: 99.3 us -> 94.4 us
    pallas_call x1, Pallas kernels: 99.3 us -> 94.4 us  [shards(): pl.pallas_call(functools.partial(kernel, sizes), out_shape=jax.ShapeDtype...]
where the time goes in v3:
time: 98.4 us; the launch traced here: 96.5 us
  Pallas kernels  94.4 us (96%)
  local copies, waits for them, and re-layouts  2.1 us (2%)
    pallas_call x1, Pallas kernels, shards(): pl.pallas_call(functools.partial(kernel, sizes), out_shape=jax.ShapeDtype...  94.4 us
    unnamed x1, local copies, waits for them, and re-layouts  2.1 us

profile of v3, /device:TPU:1, one launch (start us, length us, event | category | flops | bytes accessed | tf_op | source)
XLA Modules:
  0.0 96.5 jit_solution(1511205166696037380)
XLA Ops:
  0.0 94.4 %shard_map.145 = f32[2,3,64,512]{3,2,1,0:T(8,128)} custom-call(f32[3]{0:T(128)} %thr.1, f32[2,3,64,512]{3,2,1,0:T(8,128)} %refs_0_.1, f32[2,2,3,64,512]{4,3,2,1,0:T(8,128)} %refs_1_.1, f32[2,2,3,64,512]{4,3,2,1,0:T(8,128)} %refs_2_.1, s32[64,512]{1,0:T(8,128)} %refs_3_.1, bf16[2,512,512]{2,1,0:T(8,128)(2,1)} %constant.20.clone.refs_4_, ...), custom_call_target="tpu_custom_call" | custom-call | tf_op jit(solution)/shard_map/pallas_call | solution.py:350
  94.4 2.1 %copy.17 = f32[2,3,64,512]{3,2,1,0:T(8,128)} copy(f32[2,3,64,512]{3,2,1,0:T(8,128)} %shard_map.145) | data formatting | bytes 1572864

commit v4 on v3

--- a/solution.py
+++ b/solution.py
@@ -240,11 +240,11 @@
             total = total + pieces[r, g]
         moved = image[:, r, cut_of(group), :] - total
         window[r, :, pl.ds(pl.multiple_of(HALO + start_of(group), 8), piece), :] = moved
+        if fold:
+            edges(r, lambda copy: copy.start())
         if piece < rows:
             for k in range(1, groups):
                 spread(r, k).start()
-        if fold:
-            edges(r, lambda copy: copy.start())
 
     def stage_edges(r):
         if fold:

time: 98.4 us -> 98.4 us (level)
  no operation moved by 1% of the time
where the time goes in v4:
time: 98.4 us; the launch traced here: 96.5 us
  Pallas kernels  94.4 us (96%)
  local copies, waits for them, and re-layouts  2.1 us (2%)
    pallas_call x1, Pallas kernels, shards(): pl.pallas_call(functools.partial(kernel, sizes), out_shape=jax.ShapeDtype...  94.4 us
    unnamed x1, local copies, waits for them, and re-layouts  2.1 us

profile of v4, /device:TPU:1, one launch (start us, length us, event | category | flops | bytes accessed | tf_op | source)
XLA Modules:
  0.0 96.5 jit_solution(7837994650127734777)
XLA Ops:
  0.0 94.4 %shard_map.145 = f32[2,3,64,512]{3,2,1,0:T(8,128)} custom-call(f32[3]{0:T(128)} %thr.1, f32[2,3,64,512]{3,2,1,0:T(8,128)} %refs_0_.1, f32[2,2,3,64,512]{4,3,2,1,0:T(8,128)} %refs_1_.1, f32[2,2,3,64,512]{4,3,2,1,0:T(8,128)} %refs_2_.1, s32[64,512]{1,0:T(8,128)} %refs_3_.1, bf16[2,512,512]{2,1,0:T(8,128)(2,1)} %constant.20.clone.refs_4_, ...), custom_call_target="tpu_custom_call" | custom-call | tf_op jit(solution)/shard_map/pallas_call | solution.py:350
  94.4 2.1 %copy.17 = f32[2,3,64,512]{3,2,1,0:T(8,128)} copy(f32[2,3,64,512]{3,2,1,0:T(8,128)} %shard_map.145) | data formatting | bytes 1572864
